TPU v7x, 32 devices: a whole 2x2x4 slice. The times are simulated.
32 devices in a mesh: grp: 2 (over y), tile: 4 (over z), var: 4 (over x, core).
Axes of the slice: x: 2, y: 2, z: 4, core: 2. Of those that a mesh axis runs over, the one named last changes fastest.
Arguments:
- control: float32 [8, 128, 2048], P('var', ('grp', 'tile')), parts along dimension 1, may hold values from -6 to 6
- diffusivity: float32 [2, 128, 2048], P(None, ('grp', 'tile')), parts along dimension 1, may hold values from 0.05 to 0.95
- land_mask: int32 [128, 2048], P(('grp', 'tile')), parts along dimension 0, may hold values 0 or 1
- panel_tile: int32 [1024, 1], P(('grp', 'tile')), parts along dimension 0, may hold values from 0 to 3; in each aligned block of 128 rows (0 to 127, 128 to 255, ...) at most 64 rows name the same one
- panel_row: int32 [1024], P(('grp', 'tile')), parts along dimension 0, may hold values from 0 to 15
- panel_cols: int32 [1024, 128], P(('grp', 'tile')), parts along dimension 0, may hold values from 0 to 2047
- obs_values: float32 [1024, 128], P(('grp', 'tile')), parts along dimension 0, may hold values from -6 to 6
- obs_weights: float32 [1024, 128], P(('grp', 'tile')), parts along dimension 0, may hold values from 0.5 to 4
- panel_sensor: int32 [1024], P(('grp', 'tile')), parts along dimension 0, may hold values from 0 to 1
- sensitivity: float32 [2, 8], replicated, may hold values from 0.2 to 1
- cross_factor: float32 [8, 8], replicated, may hold values from -0.45 to 2
Outputs:
- gradient: float32 [8, 128, 2048], P('var', ('grp', 'tile')), parts along dimension 1
There are 2 independent parts, one for each index of `grp`. A program takes and returns all parts, laid end to end along the dimension named above; an argument that names none is the same for every part. Nothing has to cross between parts.
Inputs may be any that keep to these rules, and one draw needn't show every extreme that they name: `panel_tile`: among the 128 panels held by one tile index, at most 64 name the same tile.
All inputs are finite; a program needn't handle non-finite values. No bound on the sum of `land_mask` on one device may be relied on, other than what follows from the above.
Results may differ from a plain program's by a relative error of at most 0.00014.
Values sent between devices are 32-bit elements; how exact they have to be, the bound alone decides.
No kernel may reach another device: no remote copies, remote signals or barrier semaphores. Data moves between devices by JAX's collectives and lax.ppermute only.
A program may use at most 128 MiB of HBM per device.

v0:
```python
import functools

import jax
import jax.numpy as jnp
from jax import lax
from jax.experimental import pallas as pl
from jax.experimental.pallas import tpu as pltpu
from jax.sharding import PartitionSpec as P

PASSES = 10
LANES = 128
GROUP = 16
VMEM = pl.BlockSpec(memory_space=pltpu.VMEM)
SMEM = pl.BlockSpec(memory_space=pltpu.SMEM)
HBM = pl.BlockSpec(memory_space=pltpu.HBM)
AFTER = pl.BlockSpec(memory_space=pl.ANY)
F32 = jnp.float32


def in_hbm(values):
    return pltpu.with_memory_space_constraint(values, pltpu.HBM)


def call(body, outs, ins, scratch=(), limit=16, cost=None):
    return pl.pallas_call(
        body,
        out_shape=outs,
        in_specs=ins,
        out_specs=[VMEM] * len(outs),
        scratch_shapes=list(scratch),
        compiler_params=pltpu.CompilerParams(vmem_limit_bytes=limit << 20),
        cost_estimate=cost,
    )


def cost(cycles):
    return pl.CostEstimate(flops=cycles * 4096, bytes_accessed=cycles * 1024, transcendentals=0)


def response(sens_ref, factor_ref, sensor, variable):
    total = sens_ref[sensor, 0] * factor_ref[0, variable]
    for u in range(1, factor_ref.shape[0]):
        total = total + sens_ref[sensor, u] * factor_ref[u, variable]
    return total


def fetch(pairs, sems):
    copies = [pltpu.make_async_copy(src, dst, sems.at[i]) for i, (src, dst) in enumerate(pairs)]
    for copy in copies:
        copy.start()
    return copies


def first_kernel(slots, margin, sens_hbm, factor_hbm, control_hbm, kappa_hbm, tile_hbm, row_hbm, sensor_hbm,
                 value_hbm, weight_hbm, cols_hbm, own_ref, other_ref, response_ref, kappa_ref, even_ref,
                 odd_ref, *refs):
    chunk_refs = refs[:-12]
    (sens_ref, factor_ref, control_ref, tile_ref, row_ref, sensor_ref, value_ref, weight_ref, cols_ref,
     send_ref, count_ref, sems) = refs[-12:]
    pairs = (
        (sens_hbm, sens_ref), (factor_hbm, factor_ref), (control_hbm, control_ref),
        (kappa_hbm, kappa_ref), (tile_hbm, tile_ref), (row_hbm, row_ref), (sensor_hbm, sensor_ref),
        (value_hbm, value_ref), (weight_hbm, weight_ref), (cols_hbm, cols_ref),
    )
    copies = [pltpu.make_async_copy(src, dst, sems.at[i]) for i, (src, dst) in enumerate(pairs)]
    for copy in copies:
        copy.start()
    send_ref[...] = jnp.zeros(send_ref.shape, F32)
    turns = len(chunk_refs)
    for turn in range(turns):
        count_ref[turn] = 0
    for copy in copies:
        copy.wait()

    member, mine = lax.axis_index("var"), lax.axis_index("tile")
    core = member % 2
    var_dev = control_ref.shape[0]
    for which, (sensor, out_ref) in enumerate(((core, own_ref), (1 - core, other_ref))):
        total = None
        for v in range(var_dev):
            scale = response(sens_ref, factor_ref, sensor, member * var_dev + v)
            response_ref[which, v] = jnp.full(response_ref.shape[2:], scale, F32)
            term = scale * control_ref[v]
            total = term if total is None else total + term
        out_ref[...] = total
    pack_edges(even_ref, odd_ref, jnp.where(core == 0, kappa_ref[0], kappa_ref[1]), margin)

    panels = value_ref.shape[0]
    sub = lax.broadcasted_iota(jnp.int32, (8 * turns, LANES), 0)
    lane = lax.broadcasted_iota(jnp.int32, (8 * turns, LANES), 1)
    trash = 3 * slots + 7

    def place(p, meta):
        turn = (tile_ref[p] ^ mine) - core * turns
        keep = (turn >= 0) & (turn < turns)
        turn = jnp.where(keep, turn, 0)
        slot = count_ref[turn]
        count_ref[turn] = slot + keep.astype(jnp.int32)
        rows = (value_ref[pl.ds(p, 1), :], weight_ref[pl.ds(p, 1), :], cols_ref[pl.ds(p, 1), :].astype(F32))
        for part, row in enumerate(rows):
            send_ref[turn, pl.ds(jnp.where(keep, part * slots + slot, trash), 1), :] = row
        facts = jnp.where(sub == 8 * turn, row_ref[p], sensor_ref[p]).astype(F32)
        here = (lane == jnp.where(keep, slot, LANES)) & (sub // 8 == turn)
        return jnp.where(here, facts, meta)

    meta = lax.fori_loop(0, panels, place, jnp.zeros((8 * turns, LANES), F32), unroll=8)
    for turn, chunk_ref in enumerate(chunk_refs):
        chunk_ref[: 3 * slots] = send_ref[turn, : 3 * slots]
        facts = meta[8 * turn : 8 * turn + 8]
        chunk_ref[3 * slots :] = jnp.where(lane[:8] == slots, count_ref[turn].astype(F32), facts)


def pieces(values):
    top = values.astype(jnp.bfloat16).astype(F32)
    return top, values - top


def scatter_kernel(slots, after_ref, home_ref, *refs):
    got_refs, (own_ref, other_ref, first_ref, acc_ref, meta_ref, sems) = refs[:-6], refs[-6:]
    core = lax.axis_index("var") % 2
    first_ref[...] = jnp.where(core == 0, home_ref[...], got_refs[0][...])
    got_refs = (first_ref, *got_refs[1:])
    copies = [
        pltpu.make_async_copy(ref.at[pl.ds(3 * slots, 8)], meta_ref.at[pl.ds(8 * s, 8)], sems.at[s])
        for s, ref in enumerate(got_refs)
    ]
    for copy in copies:
        copy.start()
    rows, width_cols = own_ref.shape[1:]
    blocks = width_cols // LANES
    acc_ref[...] = jnp.zeros(acc_ref.shape, F32)
    block_ids = lax.broadcasted_iota(jnp.int32, (blocks, LANES), 0)
    lane_ids = lax.broadcasted_iota(jnp.int32, (LANES, LANES), 0).astype(F32).astype(jnp.bfloat16)
    one, zero = jnp.bfloat16(1), jnp.bfloat16(0)
    sub = lax.broadcasted_iota(jnp.int32, (GROUP, LANES), 0)
    for copy in copies:
        copy.wait()

    def source(s, got_ref):
        count = meta_ref[8 * s, slots].astype(jnp.int32)

        def group(g, carry):
            base = pl.multiple_of(g * GROUP, GROUP)
            value = got_ref[pl.ds(base, GROUP), :]
            weight = got_ref[pl.ds(slots + base, GROUP), :]
            cell = got_ref[pl.ds(2 * slots + base, GROUP), :].astype(jnp.int32)
            weight = jnp.where(sub + base < count, weight, 0.0)
            parts = pieces(weight) + pieces(weight * value)
            low = (cell % LANES).astype(F32)
            high = cell // LANES
            blank = jnp.zeros((4 * blocks, LANES), jnp.bfloat16)
            for k in range(0, GROUP, 2):
                left, right = [], []
                for i in (k, k + 1):
                    in_block = block_ids == high[i : i + 1]
                    rows_of = [jnp.where(in_block, parts[j][i : i + 1], 0.0) for j in (0, 2, 1, 3)]
                    left.append(jnp.concatenate(rows_of, axis=0).astype(jnp.bfloat16))
                    column = jnp.broadcast_to(low[i : i + 1], (16, LANES)).astype(jnp.bfloat16)
                    column = jnp.concatenate([column] * (LANES // 16), axis=0)
                    right.append(jnp.where(lane_ids == column, one, zero))
                left = jnp.concatenate(
                    [
                        jnp.concatenate([left[0], blank], axis=1),
                        jnp.concatenate([blank, left[1]], axis=1),
                    ],
                    axis=0,
                )
                both = lax.dot_general(
                    left, jnp.concatenate(right, axis=1), (((1,), (1,)), ((), ())),
                    preferred_element_type=F32,
                )
                for i in (0, 1):
                    row = meta_ref[8 * s, base + k + i].astype(jnp.int32)
                    sensor = meta_ref[8 * s + 1, base + k + i].astype(jnp.int32)
                    at = pl.multiple_of((sensor * rows + row) * 2 * blocks, 2 * blocks)
                    mine = both[i * 4 * blocks : (i + 1) * 4 * blocks]
                    acc_ref[pl.ds(at, 2 * blocks), :] += mine[: 2 * blocks] + mine[2 * blocks :]
            return carry

        lax.fori_loop(0, (count + GROUP - 1) // GROUP, group, 0)

    for s, got_ref in enumerate(got_refs):
        source(s, got_ref)
    for sensor, out_ref in ((core, own_ref), (1 - core, other_ref)):
        start = sensor * rows * 2 * blocks
        for kind in range(2):
            for b in range(blocks):
                out_ref[kind, :, b * LANES : (b + 1) * LANES] = acc_ref[
                    pl.ds(start + kind * blocks + b, rows, stride=2 * blocks), :
                ]


def even_tile():
    return lax.axis_index("tile") % 2 == 0


def has_above():
    return lax.axis_index("tile") > 0


def has_below():
    return lax.axis_index("tile") + 1 < lax.axis_size("tile")


def pack_edges(even_ref, odd_ref, rows_value, margin):
    rows, width = rows_value.shape
    even = even_tile()
    for b in range(width // LANES):
        at = slice(b * LANES, (b + 1) * LANES)
        head, tail = rows_value[:margin, at], rows_value[rows - margin :, at]
        even_ref[b * margin : (b + 1) * margin] = jnp.where(even, tail, head)
        odd_ref[b * margin : (b + 1) * margin] = jnp.where(even, head, tail)


def sum_kernel(own_ref, other_ref, kappa_even_ref, kappa_odd_ref, part_ref, kappa_ref):
    kappa_ref[0] = kappa_even_ref[...]
    kappa_ref[1] = kappa_odd_ref[...]
    part_ref[...] = own_ref[...] + other_ref[...]


def edges_kernel(margin, first_ref, second_ref, *refs):
    total_ref, even_ref, odd_ref = refs[-3:]
    total = first_ref[...] + second_ref[...]
    total_ref[...] = total
    pack_edges(even_ref, odd_ref, total, margin)


def ring_rows(rows, margin):
    return -(-(rows + 2 * margin) // 8) * 8


def lay_ring(ref, own, from_even, from_odd, margin):
    rows, total = own.shape[0], ref.shape[0]
    even = even_tile()
    ref[rows:total] = jnp.zeros((total - rows, ref.shape[1]), F32)
    ref[:rows] = own
    for b in range(ref.shape[1] // LANES):
        at = slice(b * LANES, (b + 1) * LANES)
        one, two = (m[b * margin : (b + 1) * margin] for m in (from_even, from_odd))
        ref[rows : rows + margin, at] = jnp.where(has_below(), jnp.where(even, one, two), 0.0)
        ref[total - margin :, at] = jnp.where(has_above(), jnp.where(even, two, one), 0.0)


def block(ref, j):
    return ref[:, j * LANES : (j + 1) * LANES]


def sideways(blocks):
    shape = blocks[0].shape
    lane = lax.broadcasted_iota(jnp.int32, shape, 1)
    zero = jnp.zeros(shape, F32)
    ahead = [pltpu.roll(x, 1, 1) for x in blocks]
    back = [pltpu.roll(x, LANES - 1, 1) for x in blocks]
    for j, here in enumerate(blocks):
        before = ahead[j - 1] if j else zero
        after = back[j + 1] if j + 1 < len(blocks) else zero
        yield here, jnp.where(lane == 0, before, ahead[j]), jnp.where(lane == LANES - 1, after, back[j])


def face_weights(coef_ref, row_ref, col_ref, rows, margin):
    total, width = row_ref.shape
    blocks = width // LANES
    r = lax.broadcasted_iota(jnp.int32, (total, LANES), 0)
    inside = (
        (r < rows)
        | ((r < rows + margin) & has_below())
        | ((r >= total - margin) & has_above())
    )
    scale = jnp.where(inside, 0.125, 0.0)
    unit = jnp.where(inside, 1.0, 0.0)
    columns = [block(col_ref, j) for j in range(blocks)]
    for j, (k_col, k_left, k_right) in enumerate(sideways(columns)):
        at = slice(j * LANES, (j + 1) * LANES)
        k_row = block(row_ref, j)
        up = scale * (k_row + pltpu.roll(k_row, 1, 0))
        down = scale * (k_row + pltpu.roll(k_row, total - 1, 0))
        left = scale * (k_col + k_left)
        right = scale * (k_col + k_right)
        coef_ref[0, :, at] = unit - up - down - left - right
        coef_ref[1, :, at] = up
        coef_ref[2, :, at] = down
        coef_ref[3, :, at] = left
        coef_ref[4, :, at] = right


def one_pass(source_ref, target_ref, coef_ref, spans, keep):
    width = source_ref.shape[1]

    def read(ref, *lead, at):
        got = [ref[(*lead, span, at)] for span in spans]
        return jnp.concatenate(got, axis=0) if len(got) > 1 else got[0]

    sections = [slice(j * LANES, (j + 1) * LANES) for j in range(width // LANES)]
    fields = [read(source_ref, at=at) for at in sections]
    total = fields[0].shape[0]
    for at, (here, left, right) in zip(sections, sideways(fields)):
        new = (
            read(coef_ref, 0, at=at) * here
            + read(coef_ref, 1, at=at) * pltpu.roll(here, 1, 0)
            + read(coef_ref, 2, at=at) * pltpu.roll(here, total - 1, 0)
            + read(coef_ref, 3, at=at) * left
            + read(coef_ref, 4, at=at) * right
        )
        start = 0
        for span in spans[:keep]:
            size = span.stop - span.start
            target_ref[span, at] = new[start : start + size]
            start += size


def diffuse(one_ref, two_ref, coef_ref, rows, margin):
    total = one_ref.shape[0]
    wide = [slice(0, total)]
    inner = margin // 8 * 8
    narrow = [slice(0, rows), slice(rows, rows + inner), slice(total - inner, total)]
    first = (margin - inner + 1) // 2

    def twice(spans, index, carry):
        one_pass(one_ref, two_ref, coef_ref, spans, len(spans))
        one_pass(two_ref, one_ref, coef_ref, spans, len(spans))
        return carry

    for i in range(first):
        twice(wide, i, 0)
    lax.fori_loop(0, PASSES // 2 - first - 1, functools.partial(twice, narrow), 0)
    one_pass(one_ref, two_ref, coef_ref, narrow, 3)
    one_pass(two_ref, one_ref, coef_ref, narrow, 1)


def faces_kernel(margin, mine_ref, theirs_ref, kappa_ref, sums_ref, *refs):
    coef_ref, sums_out, one_ref, two_ref = refs[-4:]
    sums_out[...] = sums_ref[...]
    rows = kappa_ref.shape[1]
    core = lax.axis_index("var") % 2
    for i, ring_ref in enumerate((one_ref, two_ref)):
        even, odd = (jnp.where(core == i, mine_ref[j], theirs_ref[j]) for j in range(2))
        lay_ring(ring_ref, kappa_ref[i], even, odd, margin)
    face_weights(coef_ref, one_ref, two_ref, rows, margin)


def smooth_kernel(margin, own_ref, even_ref, odd_ref, coef_ref, out_ref, one_ref, two_ref):
    rows = own_ref.shape[0]
    lay_ring(one_ref, own_ref[...], even_ref, odd_ref, margin)
    diffuse(one_ref, two_ref, coef_ref, rows, margin)
    out_ref[...] = one_ref[:rows]


def adjoint_kernel(margin, smooth_ref, mask_ref, sums_ref, more_ref, adjoint_ref, even_ref, odd_ref):
    weight = sums_ref[0] + more_ref[0]
    value = sums_ref[1] + more_ref[1]
    adjoint = mask_ref[...].astype(F32) * (weight * smooth_ref[...] - value)
    adjoint_ref[...] = adjoint
    pack_edges(even_ref, odd_ref, adjoint, margin)


def spread_kernel(margin, own_ref, even_ref, odd_ref, coef_ref, out_ref, one_ref, two_ref):
    rows = own_ref.shape[0]
    lay_ring(one_ref, own_ref[...], even_ref, odd_ref, margin)
    diffuse(one_ref, two_ref, coef_ref, rows, margin)
    out_ref[...] = one_ref[:rows]


def result_kernel(response_ref, control_ref, own_ref, other_ref, out_ref):
    for v in range(control_ref.shape[0]):
        mine, theirs = (response_ref[i, v][:1, :1] for i in range(2))
        out_ref[v] = control_ref[v] + mine * own_ref[...] + theirs * other_ref[...]


def swap(values, axis, bit):
    count = lax.axis_size(axis)
    return lax.ppermute(values, axis, [(i, i ^ bit) for i in range(count)])


def swap_edges(even, odd):
    tiles, members = lax.axis_size("tile"), lax.axis_size("var")
    pairs = []
    for t in range(tiles):
        other = t + 1 if t % 2 else t - 1
        for q in range(members):
            to = other * members + q if 0 <= other < tiles else t * members + (q ^ 1)
            pairs.append((t * members + q, to))
    return swap(even, "tile", 1), lax.ppermute(odd, ("tile", "var"), pairs)


def combine(values, members, first):
    bit = first
    while 2 * bit < members:
        values = values + swap(values, "var", bit)
        bit *= 2
    return values, swap(values, "var", bit)


def deliver(chunk, turn):
    tiles, members = lax.axis_size("tile"), lax.axis_size("var")
    pairs = []
    for t in range(tiles):
        for q in range(members):
            offset = (q % 2) * (tiles // 2) + turn
            pairs.append((t * members + q, (t ^ max(offset, 1)) * members + q))
    return lax.ppermute(chunk, ("tile", "var"), pairs)


def local(control, diffusivity, land_mask, panel_tile, panel_row, panel_cols, obs_values,
          obs_weights, panel_sensor, sensitivity, cross_factor):
    rows, width = control.shape[1:]
    var_dev = control.shape[0]
    tiles, members = lax.axis_size("tile"), lax.axis_size("var")
    panels, panel_width = panel_cols.shape
    slots = 2 * panels // tiles
    turns = tiles // 2
    blocks = width // LANES
    margin = PASSES
    total = ring_rows(rows, margin)
    field = jax.ShapeDtypeStruct((rows, width), F32)
    field2 = jax.ShapeDtypeStruct((2, rows, width), F32)
    edge = jax.ShapeDtypeStruct((margin * blocks, LANES), F32)
    edge2 = jax.ShapeDtypeStruct((2, margin * blocks, LANES), F32)
    chunk = jax.ShapeDtypeStruct((3 * slots + 8, panel_width), F32)
    ints = pltpu.SMEM((panels,), jnp.int32)

    own, other, responses, kappa, kappa_even, kappa_odd, *chunks = call(
        functools.partial(first_kernel, slots, margin),
        [field, field, jax.ShapeDtypeStruct((2, var_dev, 8, LANES), F32), field2, edge, edge]
        + [chunk] * turns,
        [HBM] * 10,
        [
            pltpu.SMEM(sensitivity.shape, F32),
            pltpu.SMEM(cross_factor.shape, F32),
            pltpu.VMEM(control.shape, F32),
            ints, ints, ints,
            pltpu.VMEM(obs_values.shape, F32),
            pltpu.VMEM(obs_weights.shape, F32),
            pltpu.VMEM(panel_cols.shape, jnp.int32),
            pltpu.VMEM((turns, *chunk.shape), F32),
            pltpu.SMEM((turns,), jnp.int32),
            pltpu.SemaphoreType.DMA((10,)),
        ],
        cost=cost(3000),
    )(*(in_hbm(x) for x in (sensitivity, cross_factor, control, diffusivity, panel_tile.reshape(-1),
                            panel_row, panel_sensor, obs_values, obs_weights, panel_cols)))

    got = [deliver(c, turn) for turn, c in enumerate(chunks)]
    part, kappa_mine = call(sum_kernel, [field, edge2], [VMEM] * 4, cost=cost(200))(
        own, swap(other, "var", 1), *swap_edges(kappa_even, kappa_odd)
    )
    kappa_theirs = swap(kappa_mine, "var", 1)
    part, more = combine(part, members, 2)
    smooth_in, even, odd = call(
        functools.partial(edges_kernel, margin),
        [field, edge, edge],
        [VMEM] * 2 + [AFTER] * turns,
        cost=cost(500),
    )(part, more, *got)
    even, odd = swap_edges(even, odd)
    sums, sums_other = call(
        functools.partial(scatter_kernel, slots),
        [field2, field2],
        [AFTER] + [VMEM] * (turns + 1),
        [
            pltpu.VMEM(chunk.shape, F32),
            pltpu.VMEM((2 * rows * 2 * blocks, LANES), F32),
            pltpu.SMEM((8 * turns, LANES), F32),
            pltpu.SemaphoreType.DMA((turns,)),
        ],
        cost=cost(100000),
    )(smooth_in, chunks[0], *got)
    ring = pltpu.VMEM((total, width), F32)
    coef, sums_other = call(
        functools.partial(faces_kernel, margin),
        [jax.ShapeDtypeStruct((5, total, width), F32), field2],
        [VMEM] * 4 + [AFTER] * 2,
        [ring, ring],
        cost=cost(1000),
    )(kappa_mine, kappa_theirs, kappa, sums_other, even, odd)
    more_sums = swap(sums_other, "var", 1)
    (smooth,) = call(
        functools.partial(smooth_kernel, margin),
        [field],
        [VMEM] * 4,
        [ring, ring],
        cost=cost(4000),
    )(smooth_in, even, odd, coef)
    adjoint, even, odd = call(
        functools.partial(adjoint_kernel, margin), [field, edge, edge], [VMEM] * 4, cost=cost(500)
    )(smooth, land_mask, sums, more_sums)
    even, odd = swap_edges(even, odd)
    (mine,) = call(
        functools.partial(spread_kernel, margin),
        [field],
        [VMEM] * 4,
        [ring, ring],
        cost=cost(4000),
    )(adjoint, even, odd, coef)
    (out,) = call(
        result_kernel,
        [jax.ShapeDtypeStruct(control.shape, F32)],
        [VMEM] * 4,
        cost=cost(1000),
    )(responses, control, mine, swap(mine, "var", 1))
    return out


def solution(mesh):
    return jax.shard_map(
        local,
        mesh=mesh,
        in_specs=(
            P("var", ("grp", "tile"), None),
            P(None, ("grp", "tile"), None),
            P(("grp", "tile"), None),
            P(("grp", "tile"), None),
            P(("grp", "tile")),
            P(("grp", "tile"), None),
            P(("grp", "tile"), None),
            P(("grp", "tile"), None),
            P(("grp", "tile")),
            P(),
            P(),
        ),
        out_specs=P("var", ("grp", "tile"), None),
        check_vma=False,
    )
```

profile of v0, /device:TPU:0, one launch (start us, length us, event | category | flops | bytes accessed | tf_op | source)
XLA Modules:
  0.0 35.9 jit_solution(14711673388736997208)
XLA Ops:
  0.0 2.5 %shard_map.109 = (f32[16,2048]{1,0:T(8,128)S(1)}, f32[16,2048]{1,0:T(8,128)S(1)}, f32[2,2,8,128]{3,2,1,0:T(8,128)S(1)}, f32[2,16,2048]{2,1,0:T(8,128)S(1)}, f32[...) custom-call(f32[2,8]{1,0:T(2,128)} %sens_hbm.1, ...), custom_call_target="tpu_custom_call" | custom-call | flops 12288000 | bytes 3072000 | tf_op jit(solution)/shard_map/pallas_call | solution.py:421
  2.5 0.5 %collective-permute-start = (f32[16,2048]{1,0:T(8,128)S(1)}, f32[16,2048]{1,0:T(8,128)S(1)}, u32[]{:S(2)}, u32[]{:S(2)}) collective-permute-start(f32[16,2048]{1,0:T(8,128)S(1)} %get-tuple-element.27), channel_id=1, source_target_pairs={{0,1},{1,0},{2,3},{3,2},{4,5},{5,4},{6,7},{7,6},{8,9},{9,8},{10,11... | collective-permute-start | bytes 393224 | tf_op jit(solution)/shard_map/ppermute | solution.py:371
  3.0 2.6 %collective-permute-start.1 = (f32[160,128]{1,0:T(8,128)S(1)}, f32[160,128]{1,0:T(8,128)S(1)}, u32[]{:S(2)}, u32[]{:S(2)}) collective-permute-start(f32[160,128]{1,0:T(8,128)S(1)} %get-tuple-element.28), channel_id=1, source_target_pairs={{0,4},{4,0},{8,12},{12,8},{1,5},{5,1},{9,13},{13,9},{2,6},{6,2},{1... | collective-permute-start | bytes 245768 | tf_op jit(solution)/shard_map/ppermute | solution.py:371
  5.7 0.2 collective-permute-start.2
  5.8 2.9 %collective-permute-done.1.kappa_even_ref = f32[160,128]{1,0:T(8,128)S(1)} collective-permute-done((f32[160,128]{1,0:T(8,128)S(1)}, f32[160,128]{1,0:T(8,128)S(1)}, u32[]{:S(2)}, u32[]{:S(2)}) %collective-permute-start.1) | collective-permute-done | bytes 81952 | tf_op jit(solution)/shard_map/ppermute | solution.py:371
  8.7 0.0 collective-permute-done.2.kappa_odd_ref
  8.7 1.7 %collective-permute-start.3 = (f32[16,2048]{1,0:T(8,128)S(1)}, f32[16,2048]{1,0:T(8,128)S(1)}, u32[]{:S(2)}, u32[]{:S(2)}) collective-permute-start(f32[16,2048]{1,0:T(8,128)S(1)} %get-tuple-element.30.first_ref), channel_id=1, source_target_pairs={{0,2},{1,3},{2,0},{3,1},{4,6},{5,7},{6,4},{7,5},{8,10},{9,11},{10,... | collective-permute-start | bytes 393224 | tf_op jit(solution)/shard_map/ppermute | solution.py:371
  10.5 2.7 %collective-permute-start.5 = (f32[200,128]{1,0:T(8,128)S(1)}, f32[200,128]{1,0:T(8,128)S(1)}, u32[]{:S(2)}, u32[]{:S(2)}) collective-permute-start(f32[200,128]{1,0:T(8,128)S(1)} %get-tuple-element.32), channel_id=1, source_target_pairs={{0,4},{1,13},{2,6},{3,15},{4,0},{5,9},{6,2},{7,11},{8,12},{9,5},{1... | collective-permute-start | bytes 307208 | tf_op jit(solution)/shard_map/ppermute | solution.py:400
  13.2 0.0 collective-permute-start.4
  13.2 0.2 collective-permute-start.8
  13.5 3.1 %collective-permute-done.5.refs_1_ = f32[200,128]{1,0:T(8,128)S(1)} collective-permute-done((f32[200,128]{1,0:T(8,128)S(1)}, f32[200,128]{1,0:T(8,128)S(1)}, u32[]{:S(2)}, u32[]{:S(2)}) %collective-permute-start.5) | collective-permute-done | bytes 102432 | tf_op jit(solution)/shard_map/ppermute | solution.py:400
  16.5 2.4 %collective-permute-done.4.refs_0_ = f32[200,128]{1,0:T(8,128)S(1)} collective-permute-done((f32[200,128]{1,0:T(8,128)S(1)}, f32[200,128]{1,0:T(8,128)S(1)}, u32[]{:S(2)}, u32[]{:S(2)}) %collective-permute-start.4) | collective-permute-done | bytes 102432 | tf_op jit(solution)/shard_map/ppermute | solution.py:400
  18.9 0.0 collective-permute-done.3.second_ref
  19.0 1.6 %collective-permute-start.6 = (f32[160,128]{1,0:T(8,128)S(1)}, f32[160,128]{1,0:T(8,128)S(1)}, u32[]{:S(2)}, u32[]{:S(2)}) collective-permute-start(f32[160,128]{1,0:T(8,128)S(1)} %get-tuple-element.34), channel_id=1, source_target_pairs={{0,4},{4,0},{8,12},{12,8},{1,5},{5,1},{9,13},{13,9},{2,6},{6,2},{1... | collective-permute-start | bytes 245768 | tf_op jit(solution)/shard_map/ppermute | solution.py:371
  20.6 3.7 %shard_map.112 = (f32[2,16,2048]{2,1,0:T(8,128)S(1)}, f32[2,16,2048]{2,1,0:T(8,128)S(1)}) custom-call(f32[16,2048]{1,0:T(8,128)S(1)} %get-tuple-element.33.after_ref.own_ref, f32[200,128]{1,0:T(8,128)S(1)} %get-tuple-element.31.home_ref, f32[200,128]{1,0:T(8,128)S(1)} %collective-permute-done.4.refs_0_, f32[200,128]{1,0:T(8,128)S(1)} %collective-permute-done.5.refs_1_), custom_call_target="tpu_custom_call" | custom-call | flops 409600000 | bytes 102400000 | tf_op jit(solution)/shard_map/pallas_call | solution.py:455
  24.3 0.0 copy-start.1
  24.3 0.0 collective-permute-done.6.refs_0_.even_ref
  24.3 0.0 collective-permute-done.7.refs_1_.odd_ref
  24.3 0.3 shard_map.113
  24.6 0.6 %collective-permute-start.9 = (f32[2,16,2048]{2,1,0:T(8,128)S(1)}, f32[2,16,2048]{2,1,0:T(8,128)S(1)}, u32[]{:S(2)}, u32[]{:S(2)}) collective-permute-start(f32[2,16,2048]{2,1,0:T(8,128)S(1)} %get-tuple-element.41), channel_id=1, source_target_pairs={{0,1},{1,0},{2,3},{3,2},{4,5},{5,4},{6,7},{7,6},{8,9},{9,8},{10,11... | collective-permute-start | bytes 786440 | tf_op jit(solution)/shard_map/ppermute | solution.py:371
  25.2 1.9 %shard_map.114.smooth_ref = f32[16,2048]{1,0:T(8,128)S(1)} custom-call(f32[16,2048]{1,0:T(8,128)S(1)} %get-tuple-element.33.after_ref.own_ref, f32[160,128]{1,0:T(8,128)S(1)} %collective-permute-done.6.refs_0_.even_ref, f32[160,128]{1,0:T(8,128)S(1)} %collective-permute-done.7.refs_1_.odd_ref, f32[5,40,2048]{2,1,0:T(8,128)S(1)} %get-tuple-element.39.coef_ref), custom_call_target="tpu_custom_call" | custom-call | flops 16384000 | bytes 4096000 | tf_op jit(solution)/shard_map/pallas_call | solution.py:476
  27.1 0.0 copy-start
  27.1 0.0 collective-permute-done.9.more_ref
  27.2 0.1 shard_map.115
  27.2 1.3 %collective-permute-start.10 = (f32[160,128]{1,0:T(8,128)S(1)}, f32[160,128]{1,0:T(8,128)S(1)}, u32[]{:S(2)}, u32[]{:S(2)}) collective-permute-start(f32[160,128]{1,0:T(8,128)S(1)} %get-tuple-element.43), channel_id=1, source_target_pairs={{0,4},{4,0},{8,12},{12,8},{1,5},{5,1},{9,13},{13,9},{2,6},{6,2},{1... | collective-permute-start | bytes 245768 | tf_op jit(solution)/shard_map/ppermute | solution.py:371
  28.6 0.2 collective-permute-start.11
  28.8 3.0 %collective-permute-done.10.even_ref = f32[160,128]{1,0:T(8,128)S(1)} collective-permute-done((f32[160,128]{1,0:T(8,128)S(1)}, f32[160,128]{1,0:T(8,128)S(1)}, u32[]{:S(2)}, u32[]{:S(2)}) %collective-permute-start.10) | collective-permute-done | bytes 81952 | tf_op jit(solution)/shard_map/ppermute | solution.py:371
  31.7 0.0 collective-permute-done.11.odd_ref
  31.7 1.9 %shard_map.116.own_ref = f32[16,2048]{1,0:T(8,128)S(1)} custom-call(f32[16,2048]{1,0:T(8,128)S(1)} %get-tuple-element.42.own_ref, f32[160,128]{1,0:T(8,128)S(1)} %collective-permute-done.10.even_ref, f32[160,128]{1,0:T(8,128)S(1)} %collective-permute-done.11.odd_ref, f32[5,40,2048]{2,1,0:T(8,128)S(1)} %get-tuple-element.39.coef_ref), custom_call_target="tpu_custom_call" | custom-call | flops 16384000 | bytes 4096000 | tf_op jit(solution)/shard_map/pallas_call | solution.py:487
  33.7 0.1 collective-permute-start.12
  33.8 1.3 %collective-permute-done.12.other_ref = f32[16,2048]{1,0:T(8,128)S(1)} collective-permute-done((f32[16,2048]{1,0:T(8,128)S(1)}, f32[16,2048]{1,0:T(8,128)S(1)}, u32[]{:S(2)}, u32[]{:S(2)}) %collective-permute-start.12) | collective-permute-done | bytes 131104 | tf_op jit(solution)/shard_map/ppermute | solution.py:371
  35.1 0.8 %shard_map.117 = f32[2,16,2048]{2,1,0:T(8,128)} custom-call(f32[2,2,8,128]{3,2,1,0:T(8,128)S(1)} %get-tuple-element.25.response_ref, f32[2,16,2048]{2,1,0:T(8,128)S(1)} %copy-done, f32[16,2048]{1,0:T(8,128)S(1)} %shard_map.116.own_ref, f32[16,2048]{1,0:T(8,128)S(1)} %collective-permute-done.12.other_ref), custom_call_target="tpu_custom_call" | custom-call | flops 4096000 | bytes 1024000 | tf_op jit(solution)/shard_map/pallas_call | solution.py:494
  (7 shorter events, 0.1 us)
Async XLA Ops:
  2.5 6.2 %collective-permute-start = (f32[16,2048]{1,0:T(8,128)S(1)}, f32[16,2048]{1,0:T(8,128)S(1)}, u32[]{:S(2)}, u32[]{:S(2)}) collective-permute-start(f32[16,2048]{1,0:T(8,128)S(1)} %get-tuple-element.27), channel_id=1, source_target_pairs={{0,1},{1,0},{2,3},{3,2},{4,5},{5,4},{6,7},{7,6},{8,9},{9,8},{10,11... | collective-permute-start | bytes 393224 | tf_op jit(solution)/shard_map/ppermute | solution.py:371
  3.0 5.7 %collective-permute-start.1 = (f32[160,128]{1,0:T(8,128)S(1)}, f32[160,128]{1,0:T(8,128)S(1)}, u32[]{:S(2)}, u32[]{:S(2)}) collective-permute-start(f32[160,128]{1,0:T(8,128)S(1)} %get-tuple-element.28), channel_id=1, source_target_pairs={{0,4},{4,0},{8,12},{12,8},{1,5},{5,1},{9,13},{13,9},{2,6},{6,2},{1... | collective-permute-start | bytes 245768 | tf_op jit(solution)/shard_map/ppermute | solution.py:371
  5.7 3.0 %collective-permute-start.2 = (f32[160,128]{1,0:T(8,128)S(1)}, f32[160,128]{1,0:T(8,128)S(1)}, u32[]{:S(2)}, u32[]{:S(2)}) collective-permute-start(f32[160,128]{1,0:T(8,128)S(1)} %get-tuple-element.29), channel_id=1, source_target_pairs={{0,1},{1,0},{2,3},{3,2},{4,8},{5,9},{6,10},{7,11},{8,4},{9,5},{10,... | collective-permute-start | bytes 245768 | tf_op jit(solution)/shard_map/ppermute | solution.py:382
  8.7 10.2 %collective-permute-start.3 = (f32[16,2048]{1,0:T(8,128)S(1)}, f32[16,2048]{1,0:T(8,128)S(1)}, u32[]{:S(2)}, u32[]{:S(2)}) collective-permute-start(f32[16,2048]{1,0:T(8,128)S(1)} %get-tuple-element.30.first_ref), channel_id=1, source_target_pairs={{0,2},{1,3},{2,0},{3,1},{4,6},{5,7},{6,4},{7,5},{8,10},{9,11},{10,... | collective-permute-start | bytes 393224 | tf_op jit(solution)/shard_map/ppermute | solution.py:371
  10.5 6.0 %collective-permute-start.5 = (f32[200,128]{1,0:T(8,128)S(1)}, f32[200,128]{1,0:T(8,128)S(1)}, u32[]{:S(2)}, u32[]{:S(2)}) collective-permute-start(f32[200,128]{1,0:T(8,128)S(1)} %get-tuple-element.32), channel_id=1, source_target_pairs={{0,4},{1,13},{2,6},{3,15},{4,0},{5,9},{6,2},{7,11},{8,12},{9,5},{1... | collective-permute-start | bytes 307208 | tf_op jit(solution)/shard_map/ppermute | solution.py:400
  13.2 5.8 %collective-permute-start.4 = (f32[200,128]{1,0:T(8,128)S(1)}, f32[200,128]{1,0:T(8,128)S(1)}, u32[]{:S(2)}, u32[]{:S(2)}) collective-permute-start(f32[200,128]{1,0:T(8,128)S(1)} %get-tuple-element.31.home_ref), channel_id=1, source_target_pairs={{0,4},{1,9},{2,6},{3,11},{4,0},{5,13},{6,2},{7,15},{8,12},{9,1},{1... | collective-permute-start | bytes 307208 | tf_op jit(solution)/shard_map/ppermute | solution.py:400
  13.2 11.0 %collective-permute-start.8 = (f32[2,160,128]{2,1,0:T(8,128)S(1)}, f32[2,160,128]{2,1,0:T(8,128)S(1)}, u32[]{:S(2)}, u32[]{:S(2)}) collective-permute-start(f32[2,160,128]{2,1,0:T(8,128)S(1)} %get-tuple-element.36.mine_ref), channel_id=1, source_target_pairs={{0,1},{1,0},{2,3},{3,2},{4,5},{5,4},{6,7},{7,6},{8,9},{9,8},{10,11... | collective-permute-start | bytes 491528 | tf_op jit(solution)/shard_map/ppermute | solution.py:371
  19.0 5.3 %collective-permute-start.6 = (f32[160,128]{1,0:T(8,128)S(1)}, f32[160,128]{1,0:T(8,128)S(1)}, u32[]{:S(2)}, u32[]{:S(2)}) collective-permute-start(f32[160,128]{1,0:T(8,128)S(1)} %get-tuple-element.34), channel_id=1, source_target_pairs={{0,4},{4,0},{8,12},{12,8},{1,5},{5,1},{9,13},{13,9},{2,6},{6,2},{1... | collective-permute-start | bytes 245768 | tf_op jit(solution)/shard_map/ppermute | solution.py:371
  20.6 3.7 %collective-permute-start.7 = (f32[160,128]{1,0:T(8,128)S(1)}, f32[160,128]{1,0:T(8,128)S(1)}, u32[]{:S(2)}, u32[]{:S(2)}) collective-permute-start(f32[160,128]{1,0:T(8,128)S(1)} %get-tuple-element.35), channel_id=1, source_target_pairs={{0,1},{1,0},{2,3},{3,2},{4,8},{5,9},{6,10},{7,11},{8,4},{9,5},{10,... | collective-permute-start | bytes 245768 | tf_op jit(solution)/shard_map/ppermute | solution.py:382
  24.3 2.9 %copy-start.1 = (s32[16,2048]{1,0:T(8,128)S(1)}, s32[16,2048]{1,0:T(8,128)}, u32[]{:S(2)}) copy-start(s32[16,2048]{1,0:T(8,128)} %mask_ref.1) | copy-start | bytes 393220
  24.6 2.5 %collective-permute-start.9 = (f32[2,16,2048]{2,1,0:T(8,128)S(1)}, f32[2,16,2048]{2,1,0:T(8,128)S(1)}, u32[]{:S(2)}, u32[]{:S(2)}) collective-permute-start(f32[2,16,2048]{2,1,0:T(8,128)S(1)} %get-tuple-element.41), channel_id=1, source_target_pairs={{0,1},{1,0},{2,3},{3,2},{4,5},{5,4},{6,7},{7,6},{8,9},{9,8},{10,11... | collective-permute-start | bytes 786440 | tf_op jit(solution)/shard_map/ppermute | solution.py:371
  27.1 8.0 %copy-start = (f32[2,16,2048]{2,1,0:T(8,128)S(1)}, f32[2,16,2048]{2,1,0:T(8,128)}, u32[]{:S(2)}) copy-start(f32[2,16,2048]{2,1,0:T(8,128)} %control_ref.1) | copy-start | bytes 786436
  27.2 4.5 %collective-permute-start.10 = (f32[160,128]{1,0:T(8,128)S(1)}, f32[160,128]{1,0:T(8,128)S(1)}, u32[]{:S(2)}, u32[]{:S(2)}) collective-permute-start(f32[160,128]{1,0:T(8,128)S(1)} %get-tuple-element.43), channel_id=1, source_target_pairs={{0,4},{4,0},{8,12},{12,8},{1,5},{5,1},{9,13},{13,9},{2,6},{6,2},{1... | collective-permute-start | bytes 245768 | tf_op jit(solution)/shard_map/ppermute | solution.py:371
  28.6 3.2 %collective-permute-start.11 = (f32[160,128]{1,0:T(8,128)S(1)}, f32[160,128]{1,0:T(8,128)S(1)}, u32[]{:S(2)}, u32[]{:S(2)}) collective-permute-start(f32[160,128]{1,0:T(8,128)S(1)} %get-tuple-element.44), channel_id=1, source_target_pairs={{0,1},{1,0},{2,3},{3,2},{4,8},{5,9},{6,10},{7,11},{8,4},{9,5},{10,... | collective-permute-start | bytes 245768 | tf_op jit(solution)/shard_map/ppermute | solution.py:382
  33.7 1.4 %collective-permute-start.12 = (f32[16,2048]{1,0:T(8,128)S(1)}, f32[16,2048]{1,0:T(8,128)S(1)}, u32[]{:S(2)}, u32[]{:S(2)}) collective-permute-start(f32[16,2048]{1,0:T(8,128)S(1)} %shard_map.116.own_ref), channel_id=1, source_target_pairs={{0,1},{1,0},{2,3},{3,2},{4,5},{5,4},{6,7},{7,6},{8,9},{9,8},{10,11... | collective-permute-start | bytes 393224 | tf_op jit(solution)/shard_map/ppermute | solution.py:371
where the time goes:
time: 36.5 us; the launch traced here: 35.9 us
  waiting for transfers between devices  12.7 us (35%)
  starting transfers between devices  11.8 us (32%)
  Pallas kernels  11.3 us (31%)
    ppermute x8, starting transfers between devices, swap(): return lax.ppermute(values, axis, [(i, i ^ bit) for i in range(count)])  8.68 us
    ppermute x8, waiting for transfers between devices, swap(): return lax.ppermute(values, axis, [(i, i ^ bit) for i in range(count)])  7.18 us
    ppermute x2, waiting for transfers between devices, deliver(): return lax.ppermute(chunk, ('tile', 'var'), pairs)  5.47 us
    pallas_call x1, Pallas kernels, local(): call(functools.partial(scatter_kernel, slots), [field2, field2], [AFTER]...  3.68 us
    ppermute x2, starting transfers between devices, deliver(): return lax.ppermute(chunk, ('tile', 'var'), pairs)  2.74 us
    pallas_call x1, Pallas kernels, local(): call(functools.partial(first_kernel, slots, margin), [field, field, jax.S...  2.49 us
    pallas_call x1, Pallas kernels, local(): call(functools.partial(smooth_kernel, margin), [field], [VMEM] * 4, [ring...  1.94 us
    pallas_call x1, Pallas kernels, local(): call(functools.partial(spread_kernel, margin), [field], [VMEM] * 4, [ring...  1.93 us
  transfers between devices with their start and end apart: 13, of which 5 were waited for; matrix products, arithmetic and copies ran while one was open for 0% of the time, Pallas kernels for 16%

commit v1 on v0

--- a/solution.py
+++ b/solution.py
@@ -51,28 +51,23 @@
     return copies
 
 
-def first_kernel(slots, margin, sens_hbm, factor_hbm, control_hbm, kappa_hbm, tile_hbm, row_hbm, sensor_hbm,
-                 value_hbm, weight_hbm, cols_hbm, own_ref, other_ref, response_ref, kappa_ref, even_ref,
-                 odd_ref, *refs):
-    chunk_refs = refs[:-12]
-    (sens_ref, factor_ref, control_ref, tile_ref, row_ref, sensor_ref, value_ref, weight_ref, cols_ref,
-     send_ref, count_ref, sems) = refs[-12:]
-    pairs = (
-        (sens_hbm, sens_ref), (factor_hbm, factor_ref), (control_hbm, control_ref),
-        (kappa_hbm, kappa_ref), (tile_hbm, tile_ref), (row_hbm, row_ref), (sensor_hbm, sensor_ref),
-        (value_hbm, value_ref), (weight_hbm, weight_ref), (cols_hbm, cols_ref),
-    )
+def fetch(pairs, sems):
     copies = [pltpu.make_async_copy(src, dst, sems.at[i]) for i, (src, dst) in enumerate(pairs)]
     for copy in copies:
         copy.start()
-    send_ref[...] = jnp.zeros(send_ref.shape, F32)
-    turns = len(chunk_refs)
-    for turn in range(turns):
-        count_ref[turn] = 0
+    return copies
+
+
+def first_kernel(sens_hbm, factor_hbm, control_hbm, kappa_hbm, own_ref, other_ref, response_ref, kappa_ref,
+                 sens_ref, factor_ref, control_ref, sems):
+    copies = fetch(
+        ((sens_hbm, sens_ref), (factor_hbm, factor_ref), (control_hbm, control_ref),
+         (kappa_hbm, kappa_ref)),
+        sems,
+    )
     for copy in copies:
         copy.wait()
-
-    member, mine = lax.axis_index("var"), lax.axis_index("tile")
+    member = lax.axis_index("var")
     core = member % 2
     var_dev = control_ref.shape[0]
     for which, (sensor, out_ref) in enumerate(((core, own_ref), (1 - core, other_ref))):
@@ -83,31 +78,49 @@
             term = scale * control_ref[v]
             total = term if total is None else total + term
         out_ref[...] = total
-    pack_edges(even_ref, odd_ref, jnp.where(core == 0, kappa_ref[0], kappa_ref[1]), margin)
-
+
+
+def pack_kernel(slots, after_ref, tile_hbm, row_hbm, sensor_hbm, value_hbm, weight_hbm, cols_hbm, send_ref,
+                tile_ref, row_ref, sensor_ref, value_ref, weight_ref, cols_ref, count_ref, sems):
+    copies = fetch(
+        ((tile_hbm, tile_ref), (row_hbm, row_ref), (sensor_hbm, sensor_ref), (value_hbm, value_ref),
+         (weight_hbm, weight_ref), (cols_hbm, cols_ref)),
+        sems,
+    )
+    send_ref[...] = jnp.zeros(send_ref.shape, F32)
+    tiles = send_ref.shape[0]
+    for t in range(tiles):
+        count_ref[t] = 0
+    for copy in copies:
+        copy.wait()
+    core = lax.axis_index("var") % 2
     panels = value_ref.shape[0]
-    sub = lax.broadcasted_iota(jnp.int32, (8 * turns, LANES), 0)
-    lane = lax.broadcasted_iota(jnp.int32, (8 * turns, LANES), 1)
+    sub = lax.broadcasted_iota(jnp.int32, (8 * tiles, LANES), 0)
+    lane = lax.broadcasted_iota(jnp.int32, (8 * tiles, LANES), 1)
     trash = 3 * slots + 7
 
     def place(p, meta):
-        turn = (tile_ref[p] ^ mine) - core * turns
-        keep = (turn >= 0) & (turn < turns)
-        turn = jnp.where(keep, turn, 0)
-        slot = count_ref[turn]
-        count_ref[turn] = slot + keep.astype(jnp.int32)
+        t = tile_ref[p]
+        count = count_ref[t]
+        count_ref[t] = count + 1
+        keep = count % 2 == core
+        slot = count // 2
         rows = (value_ref[pl.ds(p, 1), :], weight_ref[pl.ds(p, 1), :], cols_ref[pl.ds(p, 1), :].astype(F32))
         for part, row in enumerate(rows):
-            send_ref[turn, pl.ds(jnp.where(keep, part * slots + slot, trash), 1), :] = row
-        facts = jnp.where(sub == 8 * turn, row_ref[p], sensor_ref[p]).astype(F32)
-        here = (lane == jnp.where(keep, slot, LANES)) & (sub // 8 == turn)
+            send_ref[t, pl.ds(jnp.where(keep, part * slots + slot, trash), 1), :] = row
+        facts = jnp.where(sub == 8 * t, row_ref[p], sensor_ref[p]).astype(F32)
+        here = (lane == jnp.where(keep, slot, LANES)) & (sub // 8 == t)
         return jnp.where(here, facts, meta)
 
-    meta = lax.fori_loop(0, panels, place, jnp.zeros((8 * turns, LANES), F32), unroll=8)
-    for turn, chunk_ref in enumerate(chunk_refs):
-        chunk_ref[: 3 * slots] = send_ref[turn, : 3 * slots]
-        facts = meta[8 * turn : 8 * turn + 8]
-        chunk_ref[3 * slots :] = jnp.where(lane[:8] == slots, count_ref[turn].astype(F32), facts)
+    meta = lax.fori_loop(0, panels, place, jnp.zeros((8 * tiles, LANES), F32), unroll=8)
+    for t in range(tiles):
+        facts = meta[8 * t : 8 * t + 8]
+        held = (count_ref[t] + 1 - core) // 2
+        send_ref[t, 3 * slots :] = jnp.where(lane[:8] == slots, held.astype(F32), facts)
+
+
+def relay_kernel(after_ref, in_ref, out_ref):
+    out_ref[...] = in_ref[...]
 
 
 def pieces(values):
@@ -115,11 +128,9 @@
     return top, values - top
 
 
-def scatter_kernel(slots, after_ref, home_ref, *refs):
-    got_refs, (own_ref, other_ref, first_ref, acc_ref, meta_ref, sems) = refs[:-6], refs[-6:]
+def scatter_kernel(slots, after_ref, got_ref, own_ref, other_ref, acc_ref, meta_ref, sems):
     core = lax.axis_index("var") % 2
-    first_ref[...] = jnp.where(core == 0, home_ref[...], got_refs[0][...])
-    got_refs = (first_ref, *got_refs[1:])
+    got_refs = [got_ref.at[s] for s in range(got_ref.shape[0])]
     copies = [
         pltpu.make_async_copy(ref.at[pl.ds(3 * slots, 8)], meta_ref.at[pl.ds(8 * s, 8)], sems.at[s])
         for s, ref in enumerate(got_refs)
@@ -212,17 +223,11 @@
         odd_ref[b * margin : (b + 1) * margin] = jnp.where(even, head, tail)
 
 
-def sum_kernel(own_ref, other_ref, kappa_even_ref, kappa_odd_ref, part_ref, kappa_ref):
-    kappa_ref[0] = kappa_even_ref[...]
-    kappa_ref[1] = kappa_odd_ref[...]
-    part_ref[...] = own_ref[...] + other_ref[...]
-
-
-def edges_kernel(margin, first_ref, second_ref, *refs):
-    total_ref, even_ref, odd_ref = refs[-3:]
+def edges_kernel(margin, first_ref, second_ref, kappa_ref, total_ref, even_ref, odd_ref):
     total = first_ref[...] + second_ref[...]
     total_ref[...] = total
-    pack_edges(even_ref, odd_ref, total, margin)
+    for i, field in enumerate((total, kappa_ref[0], kappa_ref[1])):
+        pack_edges(even_ref.at[i], odd_ref.at[i], field, margin)
 
 
 def ring_rows(rows, margin):
@@ -327,20 +332,17 @@
     one_pass(two_ref, one_ref, coef_ref, narrow, 1)
 
 
-def faces_kernel(margin, mine_ref, theirs_ref, kappa_ref, sums_ref, *refs):
-    coef_ref, sums_out, one_ref, two_ref = refs[-4:]
+def faces_kernel(margin, even_ref, odd_ref, kappa_ref, sums_ref, coef_ref, sums_out, one_ref, two_ref):
     sums_out[...] = sums_ref[...]
     rows = kappa_ref.shape[1]
-    core = lax.axis_index("var") % 2
-    for i, ring_ref in enumerate((one_ref, two_ref)):
-        even, odd = (jnp.where(core == i, mine_ref[j], theirs_ref[j]) for j in range(2))
-        lay_ring(ring_ref, kappa_ref[i], even, odd, margin)
+    lay_ring(one_ref, kappa_ref[0], even_ref.at[1], odd_ref.at[1], margin)
+    lay_ring(two_ref, kappa_ref[1], even_ref.at[2], odd_ref.at[2], margin)
     face_weights(coef_ref, one_ref, two_ref, rows, margin)
 
 
 def smooth_kernel(margin, own_ref, even_ref, odd_ref, coef_ref, out_ref, one_ref, two_ref):
     rows = own_ref.shape[0]
-    lay_ring(one_ref, own_ref[...], even_ref, odd_ref, margin)
+    lay_ring(one_ref, own_ref[...], even_ref.at[0], odd_ref.at[0], margin)
     diffuse(one_ref, two_ref, coef_ref, rows, margin)
     out_ref[...] = one_ref[:rows]
 
@@ -390,88 +392,81 @@
     return values, swap(values, "var", bit)
 
 
-def deliver(chunk, turn):
-    tiles, members = lax.axis_size("tile"), lax.axis_size("var")
-    pairs = []
-    for t in range(tiles):
-        for q in range(members):
-            offset = (q % 2) * (tiles // 2) + turn
-            pairs.append((t * members + q, (t ^ max(offset, 1)) * members + q))
-    return lax.ppermute(chunk, ("tile", "var"), pairs)
-
-
 def local(control, diffusivity, land_mask, panel_tile, panel_row, panel_cols, obs_values,
           obs_weights, panel_sensor, sensitivity, cross_factor):
     rows, width = control.shape[1:]
     var_dev = control.shape[0]
     tiles, members = lax.axis_size("tile"), lax.axis_size("var")
     panels, panel_width = panel_cols.shape
-    slots = 2 * panels // tiles
-    turns = tiles // 2
+    slots = panels // tiles
     blocks = width // LANES
     margin = PASSES
     total = ring_rows(rows, margin)
     field = jax.ShapeDtypeStruct((rows, width), F32)
     field2 = jax.ShapeDtypeStruct((2, rows, width), F32)
     edge = jax.ShapeDtypeStruct((margin * blocks, LANES), F32)
-    edge2 = jax.ShapeDtypeStruct((2, margin * blocks, LANES), F32)
-    chunk = jax.ShapeDtypeStruct((3 * slots + 8, panel_width), F32)
+    edge3 = jax.ShapeDtypeStruct((3, margin * blocks, LANES), F32)
+    chunks = jax.ShapeDtypeStruct((tiles, 3 * slots + 8, panel_width), F32)
     ints = pltpu.SMEM((panels,), jnp.int32)
 
-    own, other, responses, kappa, kappa_even, kappa_odd, *chunks = call(
-        functools.partial(first_kernel, slots, margin),
-        [field, field, jax.ShapeDtypeStruct((2, var_dev, 8, LANES), F32), field2, edge, edge]
-        + [chunk] * turns,
-        [HBM] * 10,
+    own, other, responses, kappa = call(
+        first_kernel,
+        [field, field, jax.ShapeDtypeStruct((2, var_dev, 8, LANES), F32), field2],
+        [HBM] * 4,
         [
             pltpu.SMEM(sensitivity.shape, F32),
             pltpu.SMEM(cross_factor.shape, F32),
             pltpu.VMEM(control.shape, F32),
+            pltpu.SemaphoreType.DMA((4,)),
+        ],
+        cost=cost(2000),
+    )(*(in_hbm(x) for x in (sensitivity, cross_factor, control, diffusivity)))
+    (send,) = call(
+        functools.partial(pack_kernel, slots),
+        [chunks],
+        [AFTER] + [HBM] * 6,
+        [
             ints, ints, ints,
             pltpu.VMEM(obs_values.shape, F32),
             pltpu.VMEM(obs_weights.shape, F32),
             pltpu.VMEM(panel_cols.shape, jnp.int32),
-            pltpu.VMEM((turns, *chunk.shape), F32),
-            pltpu.SMEM((turns,), jnp.int32),
-            pltpu.SemaphoreType.DMA((10,)),
+            pltpu.SMEM((tiles,), jnp.int32),
+            pltpu.SemaphoreType.DMA((6,)),
         ],
         cost=cost(3000),
-    )(*(in_hbm(x) for x in (sensitivity, cross_factor, control, diffusivity, panel_tile.reshape(-1),
-                            panel_row, panel_sensor, obs_values, obs_weights, panel_cols)))
-
-    got = [deliver(c, turn) for turn, c in enumerate(chunks)]
-    part, kappa_mine = call(sum_kernel, [field, edge2], [VMEM] * 4, cost=cost(200))(
-        own, swap(other, "var", 1), *swap_edges(kappa_even, kappa_odd)
-    )
-    kappa_theirs = swap(kappa_mine, "var", 1)
+    )(responses, *(in_hbm(x) for x in (panel_tile.reshape(-1), panel_row, panel_sensor, obs_values,
+                                       obs_weights, panel_cols)))
+    part = own + swap(other, "var", 1)
+    (send,) = call(relay_kernel, [chunks], [AFTER, VMEM], cost=cost(100))(part, send)
+    got = lax.all_to_all(send, "tile", split_axis=0, concat_axis=0, tiled=True)
     part, more = combine(part, members, 2)
     smooth_in, even, odd = call(
         functools.partial(edges_kernel, margin),
-        [field, edge, edge],
-        [VMEM] * 2 + [AFTER] * turns,
+        [field, edge3, edge3],
+        [VMEM] * 3,
         cost=cost(500),
-    )(part, more, *got)
+    )(part, more, kappa)
     even, odd = swap_edges(even, odd)
     sums, sums_other = call(
         functools.partial(scatter_kernel, slots),
         [field2, field2],
-        [AFTER] + [VMEM] * (turns + 1),
+        [AFTER, VMEM],
         [
-            pltpu.VMEM(chunk.shape, F32),
             pltpu.VMEM((2 * rows * 2 * blocks, LANES), F32),
-            pltpu.SMEM((8 * turns, LANES), F32),
-            pltpu.SemaphoreType.DMA((turns,)),
+            pltpu.SMEM((8 * tiles, LANES), F32),
+            pltpu.SemaphoreType.DMA((tiles,)),
         ],
         cost=cost(100000),
-    )(smooth_in, chunks[0], *got)
+    )(smooth_in, got)
+
     ring = pltpu.VMEM((total, width), F32)
     coef, sums_other = call(
         functools.partial(faces_kernel, margin),
         [jax.ShapeDtypeStruct((5, total, width), F32), field2],
-        [VMEM] * 4 + [AFTER] * 2,
+        [VMEM] * 4,
         [ring, ring],
         cost=cost(1000),
-    )(kappa_mine, kappa_theirs, kappa, sums_other, even, odd)
+    )(even, odd, kappa, sums_other)
     more_sums = swap(sums_other, "var", 1)
     (smooth,) = call(
         functools.partial(smooth_kernel, margin),

time: 36.5 us -> 37.9 us (1.038)
  starting transfers between devices: 11.8 us -> 13.2 us
  Pallas kernels: 11.3 us -> 12.1 us
  waiting for transfers between devices: 12.7 us -> 11.9 us
    all_to_all x0 -> x1, waiting for transfers between devices: none -> 6.66 us  [local(): got = lax.all_to_all(send, 'tile', split_axis=0, concat_axis=0, tiled=True)]
    ppermute x2 -> x0, waiting for transfers between devices: 5.47 us -> none  [deliver(): return lax.ppermute(chunk, ('tile', 'var'), pairs)]
    all_to_all x0 -> x1, starting transfers between devices: none -> 4.87 us  [local(): got = lax.all_to_all(send, 'tile', split_axis=0, concat_axis=0, tiled=True)]
    ppermute x2 -> x0, starting transfers between devices: 2.74 us -> none  [deliver(): return lax.ppermute(chunk, ('tile', 'var'), pairs)]
    ppermute x8 -> x6, waiting for transfers between devices: 7.18 us -> 5.22 us  [swap(): return lax.ppermute(values, axis, [(i, i ^ bit) for i in range(count)])]
    pallas_call x4 -> x5, Pallas kernels: 6.24 us -> 7.1 us  [the longest x1 2.67 us: local(): call(functools.partial(pack_kernel, slots), [chunks], [AFTER] + [HBM] * 6...]
    ppermute x8 -> x6, starting transfers between devices: 8.68 us -> 8.07 us  [swap(): return lax.ppermute(values, axis, [(i, i ^ bit) for i in range(count)])]
  transfers between devices with their start and end apart: 13 -> 9, of which waited for: 5 -> 4; matrix products, arithmetic and copies ran while one was open for 0% -> 0% of each run, Pallas kernels for 16% -> 21%
where the time goes in v1:
time: 37.9 us; the launch traced here: 37.3 us
  starting transfers between devices  13.2 us (35%)
  Pallas kernels  12.1 us (32%)
  waiting for transfers between devices  11.9 us (31%)
    ppermute x6, starting transfers between devices, swap(): return lax.ppermute(values, axis, [(i, i ^ bit) for i in range(count)])  8.07 us
    all_to_all x1, waiting for transfers between devices, local(): got = lax.all_to_all(send, 'tile', split_axis=0, concat_axis=0, tiled=True)  6.66 us
    ppermute x6, waiting for transfers between devices, swap(): return lax.ppermute(values, axis, [(i, i ^ bit) for i in range(count)])  5.22 us
    all_to_all x1, starting transfers between devices, local(): got = lax.all_to_all(send, 'tile', split_axis=0, concat_axis=0, tiled=True)  4.87 us
    pallas_call x1, Pallas kernels, local(): call(functools.partial(pack_kernel, slots), [chunks], [AFTER] + [HBM] * 6...  2.67 us
    pallas_call x1, Pallas kernels, local(): call(functools.partial(scatter_kernel, slots), [field2, field2], [AFTER,...  2.51 us
    pallas_call x1, Pallas kernels, local(): call(functools.partial(smooth_kernel, margin), [field], [VMEM] * 4, [ring...  1.93 us
    pallas_call x1, Pallas kernels, local(): call(functools.partial(spread_kernel, margin), [field], [VMEM] * 4, [ring...  1.93 us
  transfers between devices with their start and end apart: 9, of which 4 were waited for; matrix products, arithmetic and copies ran while one was open for 0% of the time, Pallas kernels for 21%

profile of v1, /device:TPU:0, one launch (start us, length us, event | category | flops | bytes accessed | tf_op | source)
XLA Modules:
  0.0 37.3 jit_solution(2245570629483069202)
XLA Ops:
  0.0 1.1 %shard_map.109 = (f32[16,2048]{1,0:T(8,128)S(1)}, f32[16,2048]{1,0:T(8,128)S(1)}, f32[2,2,8,128]{3,2,1,0:T(8,128)S(1)}, f32[2,16,2048]{2,1,0:T(8,128)S(1)}) custom-call(f32[2,8]{1,0:T(2,128)} %sens_hbm.1, f32[8,8]{1,0:T(8,128)} %factor_hbm.1, f32[2,16,2048]{2,1,0:T(8,128)} %control_ref.1, f32[2,16,2048]{2,1,0:T(8,128)} %kappa_hbm.1), custom_call_target="tpu_custom_call" | custom-call | flops 8192000 | bytes 2048000 | tf_op jit(solution)/shard_map/pallas_call | solution.py:412
  1.1 0.5 %collective-permute-start = (f32[16,2048]{1,0:T(8,128)S(1)}, f32[16,2048]{1,0:T(8,128)S(1)}, u32[]{:S(2)}, u32[]{:S(2)}) collective-permute-start(f32[16,2048]{1,0:T(8,128)S(1)} %get-tuple-element.21), channel_id=1, source_target_pairs={{0,1},{1,0},{2,3},{3,2},{4,5},{5,4},{6,7},{7,6},{8,9},{9,8},{10,11... | collective-permute-start | bytes 393224 | tf_op jit(solution)/shard_map/ppermute | solution.py:373
  1.7 1.0 %collective-permute-done = f32[16,2048]{1,0:T(8,128)S(1)} collective-permute-done((f32[16,2048]{1,0:T(8,128)S(1)}, f32[16,2048]{1,0:T(8,128)S(1)}, u32[]{:S(2)}, u32[]{:S(2)}) %collective-permute-start) | collective-permute-done | bytes 131104 | tf_op jit(solution)/shard_map/ppermute | solution.py:373
  2.7 2.9 %collective-permute-start.1 = (f32[16,2048]{1,0:T(8,128)S(1)}, f32[16,2048]{1,0:T(8,128)S(1)}, u32[]{:S(2)}, u32[]{:S(2)}) collective-permute-start(f32[16,2048]{1,0:T(8,128)S(1)} %add.3.first_ref.after_ref), channel_id=1, source_target_pairs={{0,2},{1,3},{2,0},{3,1},{4,6},{5,7},{6,4},{7,5},{8,10},{9,11},{10,... | collective-permute-start | bytes 393224 | tf_op jit(solution)/shard_map/ppermute | solution.py:373
  5.6 2.7 %shard_map.111.in_ref = f32[4,104,128]{2,1,0:T(8,128)S(1)} custom-call(f32[2,2,8,128]{3,2,1,0:T(8,128)S(1)} %get-tuple-element.19.after_ref.response_ref, s32[128]{0:T(128)} %bitcast.1, s32[128]{0:T(128)} %row_hbm.1, s32[128]{0:T(128)} %sensor_hbm.1, f32[128,128]{1,0:T(8,128)} %value_hbm.1, f32[128,128]{1,0:T(8,128)} %weight_hbm.1, s32[128,128]{1,0:T(8,128)} %cols_hbm.1), custom_call_target="tpu_custom_call" | custom-call | flops 12288000 | bytes 3072000 | tf_op jit(solution)/shard_map/pallas_call | solution.py:424
  8.3 0.7 %shard_map.112 = f32[4,104,128]{2,1,0:T(8,128)} custom-call(f32[16,2048]{1,0:T(8,128)S(1)} %add.3.first_ref.after_ref, f32[4,104,128]{2,1,0:T(8,128)S(1)} %shard_map.111.in_ref), custom_call_target="tpu_custom_call" | custom-call | flops 409600 | bytes 102400 | tf_op jit(solution)/shard_map/pallas_call | solution.py:440
  9.0 4.9 %all-to-all-start = ((f32[4,104,128]{2,1,0:T(8,128)}), f32[4,104,128]{2,1,0:T(8,128)S(1)}, u32[]{:S(2)}, u32[]{:S(2)}) async-start(f32[4,104,128]{2,1,0:T(8,128)} %shard_map.112), calls=%async_computation | async-start | bytes 425984 | tf_op jit(solution)/shard_map/all_to_all | solution.py:441
  13.8 0.0 collective-permute-done.1.second_ref
  13.8 0.1 shard_map.110
  13.9 2.1 %collective-permute-start.2 = (f32[3,160,128]{2,1,0:T(8,128)S(1)}, f32[3,160,128]{2,1,0:T(8,128)S(1)}, u32[]{:S(2)}, u32[]{:S(2)}) collective-permute-start(f32[3,160,128]{2,1,0:T(8,128)S(1)} %get-tuple-element.24), channel_id=1, source_target_pairs={{0,4},{4,0},{8,12},{12,8},{1,5},{5,1},{9,13},{13,9},{2,6},{6,2},{1... | collective-permute-start | bytes 737288 | tf_op jit(solution)/shard_map/ppermute | solution.py:373
  16.0 0.0 collective-permute-start.3
  16.0 6.7 %all-to-all-done.got_ref = f32[4,104,128]{2,1,0:T(8,128)S(1)} async-done(((f32[4,104,128]{2,1,0:T(8,128)}), f32[4,104,128]{2,1,0:T(8,128)S(1)}, u32[]{:S(2)}, u32[]{:S(2)}) %all-to-all-start) | async-done | bytes 213024 | tf_op jit(solution)/shard_map/all_to_all | solution.py:441
  22.7 2.5 %shard_map.113 = (f32[2,16,2048]{2,1,0:T(8,128)S(1)}, f32[2,16,2048]{2,1,0:T(8,128)S(1)}) custom-call(f32[16,2048]{1,0:T(8,128)S(1)} %get-tuple-element.23.after_ref.own_ref, f32[4,104,128]{2,1,0:T(8,128)S(1)} %all-to-all-done.got_ref), custom_call_target="tpu_custom_call" | custom-call | flops 409600000 | bytes 102400000 | tf_op jit(solution)/shard_map/pallas_call | solution.py:450
  25.2 0.0 collective-permute-done.2.even_ref
  25.2 0.0 collective-permute-done.3.odd_ref
  25.2 0.0 copy-start.1
  25.2 0.3 shard_map.114
  25.6 0.1 collective-permute-start.4
  25.6 1.9 %shard_map.115.smooth_ref = f32[16,2048]{1,0:T(8,128)S(1)} custom-call(f32[16,2048]{1,0:T(8,128)S(1)} %get-tuple-element.23.after_ref.own_ref, f32[3,160,128]{2,1,0:T(8,128)S(1)} %collective-permute-done.2.even_ref, f32[3,160,128]{2,1,0:T(8,128)S(1)} %collective-permute-done.3.odd_ref, f32[5,40,2048]{2,1,0:T(8,128)S(1)} %get-tuple-element.27.coef_ref), custom_call_target="tpu_custom_call" | custom-call | flops 16384000 | bytes 4096000 | tf_op jit(solution)/shard_map/pallas_call | solution.py:471
  27.6 0.0 copy-start
  27.6 0.0 collective-permute-done.4.more_ref
  27.6 0.0 copy-done.1
  27.6 0.1 shard_map.116
  27.7 2.4 %collective-permute-start.5 = (f32[160,128]{1,0:T(8,128)S(1)}, f32[160,128]{1,0:T(8,128)S(1)}, u32[]{:S(2)}, u32[]{:S(2)}) collective-permute-start(f32[160,128]{1,0:T(8,128)S(1)} %get-tuple-element.31), channel_id=1, source_target_pairs={{0,4},{4,0},{8,12},{12,8},{1,5},{5,1},{9,13},{13,9},{2,6},{6,2},{1... | collective-permute-start | bytes 245768 | tf_op jit(solution)/shard_map/ppermute | solution.py:373
  30.1 0.2 collective-permute-start.6
  30.3 2.9 %collective-permute-done.5.even_ref = f32[160,128]{1,0:T(8,128)S(1)} collective-permute-done((f32[160,128]{1,0:T(8,128)S(1)}, f32[160,128]{1,0:T(8,128)S(1)}, u32[]{:S(2)}, u32[]{:S(2)}) %collective-permute-start.5) | collective-permute-done | bytes 81952 | tf_op jit(solution)/shard_map/ppermute | solution.py:373
  33.2 0.0 collective-permute-done.6.odd_ref
  33.2 1.9 %shard_map.117.own_ref = f32[16,2048]{1,0:T(8,128)S(1)} custom-call(f32[16,2048]{1,0:T(8,128)S(1)} %get-tuple-element.30.own_ref, f32[160,128]{1,0:T(8,128)S(1)} %collective-permute-done.5.even_ref, f32[160,128]{1,0:T(8,128)S(1)} %collective-permute-done.6.odd_ref, f32[5,40,2048]{2,1,0:T(8,128)S(1)} %get-tuple-element.27.coef_ref), custom_call_target="tpu_custom_call" | custom-call | flops 16384000 | bytes 4096000 | tf_op jit(solution)/shard_map/pallas_call | solution.py:482
  35.1 0.1 collective-permute-start.7
  35.2 1.3 %collective-permute-done.7.other_ref = f32[16,2048]{1,0:T(8,128)S(1)} collective-permute-done((f32[16,2048]{1,0:T(8,128)S(1)}, f32[16,2048]{1,0:T(8,128)S(1)}, u32[]{:S(2)}, u32[]{:S(2)}) %collective-permute-start.7) | collective-permute-done | bytes 131104 | tf_op jit(solution)/shard_map/ppermute | solution.py:373
  36.5 0.0 copy-done
  36.5 0.8 %shard_map.118 = f32[2,16,2048]{2,1,0:T(8,128)} custom-call(f32[2,2,8,128]{3,2,1,0:T(8,128)S(1)} %get-tuple-element.19.after_ref.response_ref, f32[2,16,2048]{2,1,0:T(8,128)S(1)} %copy-done, f32[16,2048]{1,0:T(8,128)S(1)} %shard_map.117.own_ref, f32[16,2048]{1,0:T(8,128)S(1)} %collective-permute-done.7.other_ref), custom_call_target="tpu_custom_call" | custom-call | flops 4096000 | bytes 1024000 | tf_op jit(solution)/shard_map/pallas_call | solution.py:489
  (1 shorter events, 0.0 us)
Async XLA Ops:
  1.1 1.5 %collective-permute-start = (f32[16,2048]{1,0:T(8,128)S(1)}, f32[16,2048]{1,0:T(8,128)S(1)}, u32[]{:S(2)}, u32[]{:S(2)}) collective-permute-start(f32[16,2048]{1,0:T(8,128)S(1)} %get-tuple-element.21), channel_id=1, source_target_pairs={{0,1},{1,0},{2,3},{3,2},{4,5},{5,4},{6,7},{7,6},{8,9},{9,8},{10,11... | collective-permute-start | bytes 393224 | tf_op jit(solution)/shard_map/ppermute | solution.py:373
  2.7 11.2 %collective-permute-start.1 = (f32[16,2048]{1,0:T(8,128)S(1)}, f32[16,2048]{1,0:T(8,128)S(1)}, u32[]{:S(2)}, u32[]{:S(2)}) collective-permute-start(f32[16,2048]{1,0:T(8,128)S(1)} %add.3.first_ref.after_ref), channel_id=1, source_target_pairs={{0,2},{1,3},{2,0},{3,1},{4,6},{5,7},{6,4},{7,5},{8,10},{9,11},{10,... | collective-permute-start | bytes 393224 | tf_op jit(solution)/shard_map/ppermute | solution.py:373
  9.0 13.7 %all-to-all-start = ((f32[4,104,128]{2,1,0:T(8,128)}), f32[4,104,128]{2,1,0:T(8,128)S(1)}, u32[]{:S(2)}, u32[]{:S(2)}) async-start(f32[4,104,128]{2,1,0:T(8,128)} %shard_map.112), calls=%async_computation | async-start | bytes 425984 | tf_op jit(solution)/shard_map/all_to_all | solution.py:441
  13.9 11.3 %collective-permute-start.2 = (f32[3,160,128]{2,1,0:T(8,128)S(1)}, f32[3,160,128]{2,1,0:T(8,128)S(1)}, u32[]{:S(2)}, u32[]{:S(2)}) collective-permute-start(f32[3,160,128]{2,1,0:T(8,128)S(1)} %get-tuple-element.24), channel_id=1, source_target_pairs={{0,4},{4,0},{8,12},{12,8},{1,5},{5,1},{9,13},{13,9},{2,6},{6,2},{1... | collective-permute-start | bytes 737288 | tf_op jit(solution)/shard_map/ppermute | solution.py:373
  16.0 9.2 %collective-permute-start.3 = (f32[3,160,128]{2,1,0:T(8,128)S(1)}, f32[3,160,128]{2,1,0:T(8,128)S(1)}, u32[]{:S(2)}, u32[]{:S(2)}) collective-permute-start(f32[3,160,128]{2,1,0:T(8,128)S(1)} %get-tuple-element.25), channel_id=1, source_target_pairs={{0,1},{1,0},{2,3},{3,2},{4,8},{5,9},{6,10},{7,11},{8,4},{9,5},{10,... | collective-permute-start | bytes 737288 | tf_op jit(solution)/shard_map/ppermute | solution.py:384
  25.2 2.4 %copy-start.1 = (s32[16,2048]{1,0:T(8,128)S(1)}, s32[16,2048]{1,0:T(8,128)}, u32[]{:S(2)}) copy-start(s32[16,2048]{1,0:T(8,128)} %mask_ref.1) | copy-start | bytes 393220
  25.6 2.0 %collective-permute-start.4 = (f32[2,16,2048]{2,1,0:T(8,128)S(1)}, f32[2,16,2048]{2,1,0:T(8,128)S(1)}, u32[]{:S(2)}, u32[]{:S(2)}) collective-permute-start(f32[2,16,2048]{2,1,0:T(8,128)S(1)} %get-tuple-element.29), channel_id=1, source_target_pairs={{0,1},{1,0},{2,3},{3,2},{4,5},{5,4},{6,7},{7,6},{8,9},{9,8},{10,11... | collective-permute-start | bytes 786440 | tf_op jit(solution)/shard_map/ppermute | solution.py:373
  27.6 9.0 %copy-start = (f32[2,16,2048]{2,1,0:T(8,128)S(1)}, f32[2,16,2048]{2,1,0:T(8,128)}, u32[]{:S(2)}) copy-start(f32[2,16,2048]{2,1,0:T(8,128)} %control_ref.1) | copy-start | bytes 786436
  27.7 5.5 %collective-permute-start.5 = (f32[160,128]{1,0:T(8,128)S(1)}, f32[160,128]{1,0:T(8,128)S(1)}, u32[]{:S(2)}, u32[]{:S(2)}) collective-permute-start(f32[160,128]{1,0:T(8,128)S(1)} %get-tuple-element.31), channel_id=1, source_target_pairs={{0,4},{4,0},{8,12},{12,8},{1,5},{5,1},{9,13},{13,9},{2,6},{6,2},{1... | collective-permute-start | bytes 245768 | tf_op jit(solution)/shard_map/ppermute | solution.py:373
  30.1 3.1 %collective-permute-start.6 = (f32[160,128]{1,0:T(8,128)S(1)}, f32[160,128]{1,0:T(8,128)S(1)}, u32[]{:S(2)}, u32[]{:S(2)}) collective-permute-start(f32[160,128]{1,0:T(8,128)S(1)} %get-tuple-element.32), channel_id=1, source_target_pairs={{0,1},{1,0},{2,3},{3,2},{4,8},{5,9},{6,10},{7,11},{8,4},{9,5},{10,... | collective-permute-start | bytes 245768 | tf_op jit(solution)/shard_map/ppermute | solution.py:384
  35.1 1.4 %collective-permute-start.7 = (f32[16,2048]{1,0:T(8,128)S(1)}, f32[16,2048]{1,0:T(8,128)S(1)}, u32[]{:S(2)}, u32[]{:S(2)}) collective-permute-start(f32[16,2048]{1,0:T(8,128)S(1)} %shard_map.117.own_ref), channel_id=1, source_target_pairs={{0,1},{1,0},{2,3},{3,2},{4,5},{5,4},{6,7},{7,6},{8,9},{9,8},{10,11... | collective-permute-start | bytes 393224 | tf_op jit(solution)/shard_map/ppermute | solution.py:373
